TPU v7x, 32 devices: a whole 2x2x4 slice. The times are simulated.
32 devices in a mesh: fsdp: 8 (over z, x), island: 4 (over y, core).
Axes of the slice: x: 2, y: 2, z: 4, core: 2. Of those that a mesh axis runs over, the one named last changes fastest.
Arguments:
- acts: bfloat16 [4, 2048, 4096], P('island', 'fsdp'), may hold values from -6 to 6
- grad_out: bfloat16 [4, 2048, 128], P('island', 'fsdp'), may hold values from -0.52734375 to 0.52734375
- params: float32 [4, 4096, 128], P('island', 'fsdp'), may hold values from -3 to 3
- adam_m: float32 [4, 4096, 128], P('island', 'fsdp'), may hold values from -4 to 4
- adam_v: float32 [4, 4096, 128], P('island', 'fsdp'), may hold values from 0.01 to 16
- global_params: float32 [4096, 128], P('fsdp'), may hold values from -3 to 3
- outer_mom: float32 [4096, 128], P('fsdp'), may hold values from -2 to 2
Outputs:
- mixed: float32 [4, 4096, 128], P('island', 'fsdp')
- first_moment: float32 [4, 4096, 128], P('island', 'fsdp')
- second_moment: float32 [4, 4096, 128], P('island', 'fsdp')
- new_global: float32 [4096, 128], P('fsdp')
- new_mom: float32 [4096, 128], P('fsdp')
- forward_weight: bfloat16 [4, 4096, 128], P('island')
All inputs are finite; a program needn't handle non-finite values.
Results may differ from a plain program's by a relative error of at most 0.0004.
Values may be sent and summed in bfloat16 or wider, within the bound.
A program may use at most 64 MiB of HBM per device.

v0:
```python
import jax
import jax.numpy as jnp
from jax import lax
from jax.sharding import PartitionSpec as P

INNER_STEP = 100


beta_one = 0.9
beta_two = 0.95
epsilon = 1e-08
inner_rate = 0.001
decay_rate = 0.1
outer_rate = 0.7
momentum = 0.9
mixing = 0.5


def on_device(acts, grad_out, params, adam_m, adam_v, global_params, outer_mom):
    shard_rows = params.shape[1]
    features = acts.shape[2]
    padded_rows = shard_rows * lax.axis_size("fsdp")
    islands = lax.axis_size("island")
    inputs = acts[0]
    cotangent = grad_out[0]
    whole = jnp.einsum("td,th->dh", inputs, cotangent, preferred_element_type=jnp.float32)
    whole = jnp.pad(whole, ((0, padded_rows - features), (0, 0)))
    gradient = lax.psum_scatter(whole, "fsdp", scatter_dimension=0, tiled=True)
    gradient = gradient[None]
    first_moment = beta_one * adam_m + (1.0 - beta_one) * gradient
    second_moment = beta_two * adam_v + (1.0 - beta_two) * gradient * gradient
    first_hat = first_moment / (1.0 - beta_one**INNER_STEP)
    second_hat = second_moment / (1.0 - beta_two**INNER_STEP)
    inner = params - inner_rate * (
        first_hat / (jnp.sqrt(second_hat) + epsilon) + decay_rate * params
    )
    summed = lax.psum(inner, "island")
    delta = global_params - summed[0] / islands
    new_mom = momentum * outer_mom + delta
    new_global = global_params - outer_rate * (delta + momentum * new_mom)
    mixed = mixing * inner + (1.0 - mixing) * new_global[None]
    gathered = lax.all_gather(mixed.astype(jnp.bfloat16), "fsdp", axis=1, tiled=True)
    forward_weight = gathered[:, :features]
    return (mixed, first_moment, second_moment, new_global, new_mom, forward_weight)


def solution(mesh):
    in_specs = (
        P("island", "fsdp", None),
        P("island", "fsdp", None),
        P("island", "fsdp", None),
        P("island", "fsdp", None),
        P("island", "fsdp", None),
        P("fsdp", None),
        P("fsdp", None),
    )
    out_specs = (
        P("island", "fsdp", None),
        P("island", "fsdp", None),
        P("island", "fsdp", None),
        P("fsdp", None),
        P("fsdp", None),
        P("island", None, None),
    )
    return jax.shard_map(
        on_device, mesh=mesh, in_specs=in_specs, out_specs=out_specs, check_vma=False
    )
```

profile of v0, /device:TPU:0, one launch (start us, length us, event | category | flops | bytes accessed | tf_op | source)
XLA Modules:
  0.0 168.3 jit_solution(6191435430506619618)
XLA Ops:
  7.2 0.0 copy-start
  7.2 0.0 reduce-scatter.2.cloned.1.call-start
  7.2 1.5 copy-done
  8.8 2.9 %fusion = f32[4096,128]{1,0:T(8,128)} fusion(bf16[1,256,4096]{2,1,0:T(8,128)(2,1)S(1)} %copy-done, bf16[1,256,128]{2,1,0:T(8,128)(2,1)} %param.8), kind=kOutput, calls=%fused_computation | convolution fusion | flops 268435456 | bytes 4259840 | tf_op jit(solution)/shard_map/td,th->dh/dot_general | solution.py:26
  11.7 0.0 copy-start.1
  11.7 0.0 copy-start.2
  11.7 0.0 copy-start.3
  11.7 0.0 copy-start.4
  11.7 0.0 copy-start.5
  11.7 0.0 reduce-scatter.2.cloned.1.call-update
  11.7 0.0 all-reduce.2.cloned.1.call-start
  11.8 70.7 %reduce-scatter.2.cloned.1.call-done = f32[512,128]{1,0:T(8,128)} async-done(((f32[4096,128]{1,0:T(8,128)}), f32[512,128]{1,0:T(8,128)}) %reduce-scatter.2.cloned.1.call-update) | async-done | bytes 262160 | tf_op jit(solution)/shard_map/reduce_scatter | solution.py:28
  82.4 0.0 copy-done.1
  82.4 0.0 copy-done.2
  82.5 0.0 copy-done.3
  82.5 1.9 %multiply_subtract_fusion.1 = (f32[1,512,128]{2,1,0:T(8,128)}, f32[1,512,128]{2,1,0:T(8,128)}, f32[1,512,128]{2,1,0:T(8,128)}) fusion(f32[1,512,128]{2,1,0:T(8,128)S(1)} %copy-done.1, f32[512,128]{1,0:T(8,128)} %reduce-scatter.2.cloned.1.call-done, f32[1,512,128]{2,1,0:T(8,128)S(1)} %copy-done.2, f32[1,512,128]{2,1,0:T(8,128)S(1)} %copy-done.3), kind=kLoop, calls=%fused_computation.11 | loop fusion | flops 983040 | bytes 1835008 | tf_op jit(solution)/shard_map/sub | solution.py:34
  84.4 0.0 all-reduce.2.cloned.1.call-update
  84.4 0.0 all-gather.2.cloned.1.call-start
  84.5 31.9 %all-reduce.2.cloned.1.call-done = f32[1,512,128]{2,1,0:T(8,128)} async-done(((f32[1,512,128]{2,1,0:T(8,128)}), f32[1,512,128]{2,1,0:T(8,128)}) %all-reduce.2.cloned.1.call-update) | async-done | bytes 262160 | tf_op jit(solution)/shard_map/psum | solution.py:37
  116.4 0.0 copy-done.4
  116.4 0.0 copy-done.5
  116.4 2.0 %fusion.6 = (bf16[1,512,128]{2,1,0:T(8,128)(2,1)}, f32[1,512,128]{2,1,0:T(8,128)}, f32[512,128]{1,0:T(8,128)}, f32[512,128]{1,0:T(8,128)}) fusion(f32[1,512,128]{2,1,0:T(8,128)} %get-tuple-element.10, f32[512,128]{1,0:T(8,128)S(1)} %copy-done.4, f32[1,512,128]{2,1,0:T(8,128)} %all-reduce.2.cloned.1.call-done, f32[512,128]{1,0:T(8,128)S(1)} %copy-done.5), kind=kLoop, calls=%fused_computation.13 | loop fusion | flops 720896 | bytes 1966080 | tf_op jit(solution)/shard_map/convert_element_type | solution.py:42
  118.4 0.0 all-gather.2.cloned.1.call-update
  118.4 41.1 %all-gather.2.cloned.1.call-done = bf16[1,4096,128]{2,1,0:T(8,128)(2,1)} async-done(((bf16[1,512,128]{2,1,0:T(8,128)(2,1)}), bf16[1,4096,128]{2,1,0:T(8,128)(2,1)}) %all-gather.2.cloned.1.call-update) | async-done | bytes 1048592 | tf_op jit(solution)/shard_map/all_gather | solution.py:42
  159.5 2.3 %copy.15 = bf16[1,4096,128]{2,1,0:T(8,128)(2,1)} copy(bf16[1,4096,128]{2,1,0:T(8,128)(2,1)} %all-gather.2.cloned.1.call-done) | data formatting | bytes 2097152
Async XLA Ops:
  7.2 1.6 copy-start
  7.2 75.3 %reduce-scatter.2.cloned.1.call-start = ((), (), s32[]{:S(2)}) async-start(), calls=%async_computation.1 | async-start | bytes 2359296 | tf_op jit(solution)/shard_map/reduce_scatter | solution.py:28
  11.7 70.8 %copy-start.1 = (f32[1,512,128]{2,1,0:T(8,128)S(1)}, f32[1,512,128]{2,1,0:T(8,128)}, u32[]{:S(2)}) copy-start(f32[1,512,128]{2,1,0:T(8,128)} %param.9) | copy-start | bytes 786436
  11.7 70.8 %copy-start.2 = (f32[1,512,128]{2,1,0:T(8,128)S(1)}, f32[1,512,128]{2,1,0:T(8,128)}, u32[]{:S(2)}) copy-start(f32[1,512,128]{2,1,0:T(8,128)} %param.10) | copy-start | bytes 786436
  11.7 70.8 %copy-start.3 = (f32[1,512,128]{2,1,0:T(8,128)S(1)}, f32[1,512,128]{2,1,0:T(8,128)}, u32[]{:S(2)}) copy-start(f32[1,512,128]{2,1,0:T(8,128)} %param.11) | copy-start | bytes 786436
  11.7 104.7 %copy-start.4 = (f32[512,128]{1,0:T(8,128)S(1)}, f32[512,128]{1,0:T(8,128)}, u32[]{:S(2)}) copy-start(f32[512,128]{1,0:T(8,128)} %param.12) | copy-start | bytes 786436
  11.7 104.7 %copy-start.5 = (f32[512,128]{1,0:T(8,128)S(1)}, f32[512,128]{1,0:T(8,128)}, u32[]{:S(2)}) copy-start(f32[512,128]{1,0:T(8,128)} %param.13) | copy-start | bytes 786436
  11.7 104.6 %all-reduce.2.cloned.1.call-start = ((), (), s32[]{:S(2)}) async-start(), calls=%async_computation.2 | async-start | bytes 524288 | tf_op jit(solution)/shard_map/psum | solution.py:37
  84.4 75.1 %all-gather.2.cloned.1.call-start = ((), (), s32[]{:S(2)}) async-start(), calls=%async_computation.3 | async-start | bytes 1179648 | tf_op jit(solution)/shard_map/all_gather | solution.py:42
Sparse Core Ops, SparseCore 0:
  11.9 70.5 reduce-scatter.1
  85.3 30.9 all-reduce.1
  119.3 40.1 all-gather.1
where the time goes:
time: 169 us; the launch traced here: 168 us
  waiting for transfers between devices  144 us (85%)
  between operations  13.8 us (8%)
  other arithmetic  3.95 us (2%)
  local copies, waits for them, and re-layouts  3.83 us (2%)
  matrix products  2.93 us (2%)
    reduce_scatter x1, waiting for transfers between devices, on_device(): gradient = lax.psum_scatter(whole, 'fsdp', scatter_dimension=0, tiled=True)  70.7 us
    all_gather x1, waiting for transfers between devices, on_device(): lax.all_gather(mixed.astype(jnp.bfloat16), 'fsdp', axis=1, tiled=True)  41.1 us
    psum x1, waiting for transfers between devices, on_device(): summed = lax.psum(inner, 'island')  31.9 us
    unnamed x13, local copies, waits for them, and re-layouts  3.83 us
  transfers between devices with their start and end apart: 3, of which 3 were waited for; matrix products, arithmetic and copies ran while one was open for 0% of the time, Pallas kernels for 0%

commit v1 on v0

--- a/solution.py
+++ b/solution.py
@@ -1,6 +1,10 @@
+import functools
+
 import jax
 import jax.numpy as jnp
 from jax import lax
+from jax.experimental import pallas as pl
+from jax.experimental.pallas import tpu as pltpu
 from jax.sharding import PartitionSpec as P
 
 INNER_STEP = 100
@@ -15,8 +19,251 @@
 momentum = 0.9
 mixing = 0.5
 
-
-def on_device(acts, grad_out, params, adam_m, adam_v, global_params, outer_mom):
+CODE_SCALE = 4096.0
+CHUNKS = 4
+
+
+def encode(value):
+    scaled = value * CODE_SCALE
+    return (scaled * jnp.abs(scaled) * (scaled * scaled)).astype(jnp.bfloat16)
+
+
+def decode(coded):
+    wide = coded.astype(jnp.float32)
+    size = jnp.maximum(jnp.abs(wide), 1e-37)
+    root = lax.rsqrt(lax.rsqrt(size)) * (1.0 / CODE_SCALE)
+    return jnp.where(wide < 0.0, -root, root)
+
+
+def adam(params, adam_m, adam_v, gradient):
+    first_moment = beta_one * adam_m + (1.0 - beta_one) * gradient
+    second_moment = beta_two * adam_v + (1.0 - beta_two) * gradient * gradient
+    first_hat = first_moment / (1.0 - beta_one**INNER_STEP)
+    second_hat = second_moment / (1.0 - beta_two**INNER_STEP)
+    inner = params - inner_rate * (
+        first_hat / (jnp.sqrt(second_hat) + epsilon) + decay_rate * params
+    )
+    return first_moment, second_moment, inner
+
+
+def kernel(
+    depth, pairs, chunks,
+    acts, grad_out, params, adam_m, adam_v, global_params, outer_mom,
+    mixed, first_out, second_out, new_global, new_mom, forward,
+    part, x_out, x_in, z_out, z_in, inner, core_in, y_out, y_in,
+    x_ss, x_rs, z_ss, z_rs, c_ss, c_rs, y_ss, y_rs, g_ss, g_rs, f_ss, f_rs,
+):
+    rows = params.shape[0]
+    step = rows // chunks
+    half = step // 2
+    me = lax.axis_index("fsdp")
+    isle = lax.axis_index("island")
+    zi, xi = me // 2, lax.rem(me, 2)
+    pair, core = isle // 2, lax.rem(isle, 2)
+
+    def shift(d):
+        return lax.rem(zi + d, depth)
+
+    partner = {"fsdp": zi * 2 + 1 - xi, "island": isle}
+    mate = {"fsdp": me, "island": pair * 2 + 1 - core}
+
+    def along(d):
+        return {"fsdp": shift(d) * 2 + xi, "island": isle}
+
+    def across(e, k):
+        return {"fsdp": me, "island": lax.rem(pair + e, pairs) * 2 + k}
+
+    barrier = pltpu.get_barrier_semaphore()
+    peers = [partner, mate] + [along(d) for d in range(1, depth)]
+    peers += [across(e, k) for e in range(1, pairs) for k in range(2)]
+    for peer in peers:
+        pl.semaphore_signal(barrier, inc=1, device_id=peer, device_id_type=pl.DeviceIdType.MESH)
+
+    def remote(src, dst, ss, rs, where):
+        return pltpu.make_async_remote_copy(
+            src_ref=src, dst_ref=dst, send_sem=ss, recv_sem=rs,
+            device_id=where, device_id_type=pl.DeviceIdType.MESH,
+        )
+
+    def product(block, c):
+        first = pl.multiple_of(block * rows + c * step, step)
+        return lax.dot_general(
+            acts[:, pl.ds(first, step)], grad_out[...],
+            (((0,), (0,)), ((), ())), preferred_element_type=jnp.float32,
+        )
+
+    def x_copy(c, d):
+        return remote(x_out.at[c, d], x_in.at[c, d], x_ss.at[c, d], x_rs.at[c, d], partner)
+
+    def z_copy(c, d):
+        return remote(z_out.at[c, d], z_in.at[c, d], z_ss.at[c, d], z_rs.at[c, d], along(d))
+
+    def piece(c):
+        return pl.ds(c * step, step)
+
+    def c_copy(c):
+        return remote(inner.at[piece(c)], core_in.at[c], c_ss.at[c], c_rs.at[c], mate)
+
+    def y_copy(c, e, k):
+        return remote(
+            y_out.at[c, pl.ds(pl.multiple_of(core * half, half), half)],
+            y_in.at[c, e, core], y_ss.at[c, e, k], y_rs.at[c, e, core], across(e, k),
+        )
+
+    def y_recv(c, e, k):
+        return remote(
+            y_out.at[c, pl.ds(0, half)], y_in.at[c, e, k],
+            y_ss.at[c, e, k], y_rs.at[c, e, k], mate,
+        )
+
+    def at(block, c):
+        return forward.at[pl.ds(pl.multiple_of(block * rows + c * step, step), step)]
+
+    def g_copy(c, d):
+        own = at(me, c)
+        return remote(own, own, g_ss.at[c, d], g_rs.at[c, d], partner if d == 0 else along(d))
+
+    def g_recv(c, d):
+        block = at(me if d == 0 else shift(depth - d) * 2 + xi, c)
+        return remote(block, block, g_ss.at[c, d], g_rs.at[c, d], partner)
+
+    def f_copy(c, d):
+        block = at(shift(depth - d) * 2 + xi, c)
+        return remote(block, block, f_ss.at[c, d], f_rs.at[c, d], partner)
+
+    order = list(range(1, depth)) + [0]
+
+    def x_send(c, d):
+        x_out[c, d] = encode(product(shift(d) * 2 + 1 - xi, c))
+        if c == 0 and d == order[0]:
+            pl.semaphore_wait(barrier, len(peers))
+        x_copy(c, d).start()
+
+    def z_send(c, d):
+        mine = product(shift(d) * 2 + xi, c)
+        x_copy(c, d).wait_recv()
+        z_out[c, d] = encode(mine + decode(x_in[c, d]))
+        z_copy(c, d).start()
+
+    def reduce(c):
+        part[...] = product(me, c)
+        x_copy(c, 0).wait_recv()
+        total = part[...] + decode(x_in[c, 0])
+        for d in range(1, depth):
+            z_copy(c, d).wait_recv()
+            total = total + decode(z_in[c, d])
+        s = piece(c)
+        first, second, own = adam(params[s], adam_m[s], adam_v[s], total)
+        inner[s] = own
+        c_copy(c).start()
+        first_out[s] = first
+        second_out[s] = second
+
+    def join(c):
+        c_copy(c).wait_recv()
+        y_out[c] = inner[piece(c)] + core_in[c]
+        for e in range(1, pairs):
+            for k in range(2):
+                y_copy(c, e, k).start()
+
+    def outer(c):
+        for e in range(1, pairs):
+            for k in range(2):
+                y_recv(c, e, k).wait_recv()
+        for k in range(2):
+            s = pl.ds(c * step + k * half, half)
+            summed = y_out[c, pl.ds(k * half, half)]
+            for e in range(1, pairs):
+                summed = summed + y_in[c, e, k]
+            delta = global_params[s] - summed / (2 * pairs)
+            fresh = momentum * outer_mom[s] + delta
+            moved = global_params[s] - outer_rate * (delta + momentum * fresh)
+            merged = mixing * inner[s] + (1.0 - mixing) * moved
+            first = pl.multiple_of(me * rows + c * step + k * half, half)
+            forward[pl.ds(first, half)] = merged.astype(jnp.bfloat16)
+            mixed[s] = merged
+            new_mom[s] = fresh
+            new_global[s] = moved
+        for d in order:
+            g_copy(c, d).start()
+
+    def relay(c):
+        for d in range(1, depth):
+            g_recv(c, d).wait_recv()
+            f_copy(c, d).start()
+
+    for c in range(chunks):
+        for d in order:
+            x_send(c, d)
+    for d in range(1, depth):
+        z_send(0, d)
+    for c in range(chunks):
+        after = [functools.partial(z_send, c + 1, d) for d in range(1, depth)] if c + 1 < chunks else []
+        for work in (reduce, join, outer):
+            if after:
+                after.pop(0)()
+            work(c)
+        for rest in after:
+            rest()
+        if c > 0:
+            relay(c - 1)
+    relay(chunks - 1)
+
+    for c in range(chunks):
+        c_copy(c).wait_send()
+        for e in range(1, pairs):
+            for k in range(2):
+                y_copy(c, e, k).wait_send()
+        for d in range(depth):
+            x_copy(c, d).wait_send()
+            g_copy(c, d).wait_send()
+            if d > 0:
+                z_copy(c, d).wait_send()
+                f_copy(c, d).wait_send()
+        partner_own = at(zi * 2 + 1 - xi, c)
+        remote(partner_own, partner_own, g_ss.at[c, 0], g_rs.at[c, 0], partner).wait_recv()
+        for d in range(1, depth):
+            block = at(shift(depth - d) * 2 + 1 - xi, c)
+            remote(block, block, f_ss.at[c, d], f_rs.at[c, d], partner).wait_recv()
+
+
+def fused(acts, grad_out, params, adam_m, adam_v, global_params, outer_mom):
+    fsdp, islands = lax.axis_size("fsdp"), lax.axis_size("island")
+    depth, pairs = fsdp // 2, islands // 2
+    rows, width = params.shape[1:]
+    chunks = CHUNKS
+    step = rows // chunks
+    single = jax.ShapeDtypeStruct((rows, width), jnp.float32)
+    dma = pltpu.SemaphoreType.DMA
+    vmem = pl.BlockSpec(memory_space=pltpu.VMEM)
+    coded = pltpu.VMEM((chunks, depth, step, width), jnp.bfloat16)
+    mixed, first, second, new_global, new_mom, forward = pl.pallas_call(
+        functools.partial(kernel, depth, pairs, chunks),
+        out_shape=[single] * 5 + [jax.ShapeDtypeStruct((fsdp * rows, width), jnp.bfloat16)],
+        in_specs=[vmem] * 7,
+        out_specs=[vmem] * 6,
+        scratch_shapes=[
+            pltpu.VMEM((step, width), jnp.float32),
+            coded, coded, coded, coded,
+            pltpu.VMEM((rows, width), jnp.float32),
+            pltpu.VMEM((chunks, step, width), jnp.float32),
+            pltpu.VMEM((chunks, step, width), jnp.float32),
+            pltpu.VMEM((chunks, pairs, 2, step // 2, width), jnp.float32),
+            dma((chunks, depth)), dma((chunks, depth)),
+            dma((chunks, depth)), dma((chunks, depth)),
+            dma((chunks,)), dma((chunks,)),
+            dma((chunks, pairs, 2)), dma((chunks, pairs, 2)),
+            dma((chunks, depth)), dma((chunks, depth)),
+            dma((chunks, depth)), dma((chunks, depth)),
+        ],
+        compiler_params=pltpu.CompilerParams(
+            collective_id=0, has_side_effects=True, vmem_limit_bytes=40 * 2**20
+        ),
+    )(acts[0], grad_out[0], params[0], adam_m[0], adam_v[0], global_params, outer_mom)
+    return mixed[None], first[None], second[None], new_global, new_mom, forward[None]
+
+
+def general(acts, grad_out, params, adam_m, adam_v, global_params, outer_mom):
     shard_rows = params.shape[1]
     features = acts.shape[2]
     padded_rows = shard_rows * lax.axis_size("fsdp")
@@ -26,14 +273,7 @@
     whole = jnp.einsum("td,th->dh", inputs, cotangent, preferred_element_type=jnp.float32)
     whole = jnp.pad(whole, ((0, padded_rows - features), (0, 0)))
     gradient = lax.psum_scatter(whole, "fsdp", scatter_dimension=0, tiled=True)
-    gradient = gradient[None]
-    first_moment = beta_one * adam_m + (1.0 - beta_one) * gradient
-    second_moment = beta_two * adam_v + (1.0 - beta_two) * gradient * gradient
-    first_hat = first_moment / (1.0 - beta_one**INNER_STEP)
-    second_hat = second_moment / (1.0 - beta_two**INNER_STEP)
-    inner = params - inner_rate * (
-        first_hat / (jnp.sqrt(second_hat) + epsilon) + decay_rate * params
-    )
+    first_moment, second_moment, inner = adam(params, adam_m, adam_v, gradient[None])
     summed = lax.psum(inner, "island")
     delta = global_params - summed[0] / islands
     new_mom = momentum * outer_mom + delta
@@ -44,6 +284,19 @@
     return (mixed, first_moment, second_moment, new_global, new_mom, forward_weight)
 
 
+def on_device(acts, *others):
+    fsdp, islands = lax.axis_size("fsdp"), lax.axis_size("island")
+    rows = others[1].shape[1]
+    fits = (
+        rows * fsdp == acts.shape[2]
+        and rows % (CHUNKS * 128) == 0
+        and fsdp % 2 == 0
+        and 2 <= fsdp // 2 <= 4
+        and islands == 4
+    )
+    return (fused if fits else general)(acts, *others)
+
+
 def solution(mesh):
     in_specs = (
         P("island", "fsdp", None),

time: 169 us -> 57.7 us (0.34)
  waiting for transfers between devices: 144 us -> 0 us
  Pallas kernels: 0 us -> 45 us
  between operations: 13.8 us -> 0.66 us
  local copies, waits for them, and re-layouts: 3.83 us -> 11.7 us
  other arithmetic: 3.95 us -> 0 us
  matrix products: 2.93 us -> 0 us
    reduce_scatter x1 -> x0, waiting for transfers between devices: 70.7 us -> none  [on_device(): gradient = lax.psum_scatter(whole, 'fsdp', scatter_dimension=0, tiled=True)]
    pallas_call x0 -> x1, Pallas kernels: none -> 45 us  [fused(): pl.pallas_call(functools.partial(kernel, depth, pairs, chunks), out_shape...]
    all_gather x1 -> x0, waiting for transfers between devices: 41.1 us -> none  [on_device(): lax.all_gather(mixed.astype(jnp.bfloat16), 'fsdp', axis=1, tiled=True)]
    psum x1 -> x0, waiting for transfers between devices: 31.9 us -> none  [on_device(): summed = lax.psum(inner, 'island')]
    unnamed x13 -> x20, local copies, waits for them, and re-layouts: 3.83 us -> 11.7 us
    dot_general x1 -> x0, matrix products: 2.93 us -> none  [on_device(): jnp.einsum('td,th->dh', inputs, cotangent, preferred_element_type=jnp.flo...]
    convert_element_type x1 -> x0, other arithmetic: 2.01 us -> none  [on_device(): mixed.astype(jnp.bfloat16)]
    sub x1 -> x0, other arithmetic: 1.94 us -> none  [on_device(): params - inner_rate * (first_hat / (jnp.sqrt(second_hat) + epsilon) + dec...]
  transfers between devices with their start and end apart: 3 -> 0, of which waited for: 3 -> 0; matrix products, arithmetic and copies ran while one was open for 0% -> 0% of each run, Pallas kernels for 0% -> 0%
where the time goes in v1:
time: 57.7 us; the launch traced here: 57.3 us
  Pallas kernels  45 us (78%)
  local copies, waits for them, and re-layouts  11.7 us (20%)
  between operations  0.66 us (1%)
    pallas_call x1, Pallas kernels, fused(): pl.pallas_call(functools.partial(kernel, depth, pairs, chunks), out_shape...  45 us
    unnamed x20, local copies, waits for them, and re-layouts  11.7 us

profile of v1, /device:TPU:0, one launch (start us, length us, event | category | flops | bytes accessed | tf_op | source)
XLA Modules:
  0.0 57.3 jit_solution(15461749987328720928)
XLA Ops:
  0.6 0.0 copy-start
  0.6 1.6 %copy-done = bf16[1,256,4096]{2,1,0:T(8,128)(2,1)S(1)} copy-done((bf16[1,256,4096]{2,1,0:T(8,128)(2,1)S(1)}, bf16[1,256,4096]{2,1,0:T(8,128)(2,1)}, u32[]{:S(2)}) %copy-start) | copy-done | bytes 2097176
  2.2 0.0 copy-start.1
  2.2 0.9 %copy-done.1 = f32[1,512,128]{2,1,0:T(8,128)S(1)} copy-done((f32[1,512,128]{2,1,0:T(8,128)S(1)}, f32[1,512,128]{2,1,0:T(8,128)}, u32[]{:S(2)}) %copy-start.1) | copy-done | bytes 262168
  3.2 0.0 copy-start.2
  3.2 0.9 %copy-done.2 = f32[1,512,128]{2,1,0:T(8,128)S(1)} copy-done((f32[1,512,128]{2,1,0:T(8,128)S(1)}, f32[1,512,128]{2,1,0:T(8,128)}, u32[]{:S(2)}) %copy-start.2) | copy-done | bytes 262168
  4.1 0.0 copy-start.3
  4.1 0.9 %copy-done.3 = f32[1,512,128]{2,1,0:T(8,128)S(1)} copy-done((f32[1,512,128]{2,1,0:T(8,128)S(1)}, f32[1,512,128]{2,1,0:T(8,128)}, u32[]{:S(2)}) %copy-start.3) | copy-done | bytes 262168
  5.1 0.0 copy-start.4
  5.1 0.9 %copy-done.4 = f32[512,128]{1,0:T(8,128)S(1)} copy-done((f32[512,128]{1,0:T(8,128)S(1)}, f32[512,128]{1,0:T(8,128)}, u32[]{:S(2)}) %copy-start.4) | copy-done | bytes 262168
  6.0 0.0 copy-start.5
  6.0 0.9 %copy-done.5 = f32[512,128]{1,0:T(8,128)S(1)} copy-done((f32[512,128]{1,0:T(8,128)S(1)}, f32[512,128]{1,0:T(8,128)}, u32[]{:S(2)}) %copy-start.5) | copy-done | bytes 262168
  7.0 0.0 copy-start.6
  7.0 0.8 %copy-done.6 = bf16[1,256,128]{2,1,0:T(8,128)(2,1)S(1)} copy-done((bf16[1,256,128]{2,1,0:T(8,128)(2,1)S(1)}, bf16[1,256,128]{2,1,0:T(8,128)(2,1)}, u32[]{:S(2)}) %copy-start.6) | copy-done | bytes 65560
  7.8 45.0 %shard_map.118 = (f32[512,128]{1,0:T(8,128)S(1)}, f32[512,128]{1,0:T(8,128)S(1)}, f32[512,128]{1,0:T(8,128)S(1)}, f32[512,128]{1,0:T(8,128)S(1)}, f32[512,128]{1,0:T(8,128)S(1)}, /*index=5*/bf16[4096,128]{1,0:T(8,128)(2,1)S(1)}) custom-call(bf16[256,4096]{1,0:T(8,128)(2,1)S(1)} %bitcast.9, bf16[256,128]{1,0:T(8,128)(2,1)S(1)} %bitcast.17, ...), custom_call_target="tpu_custom_call" | custom-call | tf_op jit(solution)/shard_map/pallas_call | solution.py:240
  52.9 0.7 %copy.19 = f32[1,512,128]{2,1,0:T(8,128)} copy(f32[1,512,128]{2,1,0:T(8,128)S(1)} %bitcast.13) | data formatting | bytes 524288
  53.6 0.7 %copy.20 = f32[1,512,128]{2,1,0:T(8,128)} copy(f32[1,512,128]{2,1,0:T(8,128)S(1)} %bitcast.12) | data formatting | bytes 524288
  54.3 0.7 %copy.21 = f32[1,512,128]{2,1,0:T(8,128)} copy(f32[1,512,128]{2,1,0:T(8,128)S(1)} %bitcast.11) | data formatting | bytes 524288
  55.0 0.7 %copy.22 = f32[512,128]{1,0:T(8,128)} copy(f32[512,128]{1,0:T(8,128)S(1)} %get-tuple-element.27) | data formatting | bytes 524288
  55.7 0.7 %copy.23 = f32[512,128]{1,0:T(8,128)} copy(f32[512,128]{1,0:T(8,128)S(1)} %get-tuple-element.28) | data formatting | bytes 524288
  56.4 1.0 %copy.24 = bf16[1,4096,128]{2,1,0:T(8,128)(2,1)} copy(bf16[1,4096,128]{2,1,0:T(8,128)(2,1)S(1)} %bitcast.10) | data formatting | bytes 2097152
Async XLA Ops:
  0.6 1.6 %copy-start = (bf16[1,256,4096]{2,1,0:T(8,128)(2,1)S(1)}, bf16[1,256,4096]{2,1,0:T(8,128)(2,1)}, u32[]{:S(2)}) copy-start(bf16[1,256,4096]{2,1,0:T(8,128)(2,1)} %param.7) | copy-start | bytes 6291460
  2.2 0.9 %copy-start.1 = (f32[1,512,128]{2,1,0:T(8,128)S(1)}, f32[1,512,128]{2,1,0:T(8,128)}, u32[]{:S(2)}) copy-start(f32[1,512,128]{2,1,0:T(8,128)} %param.9) | copy-start | bytes 786436
  3.2 0.9 %copy-start.2 = (f32[1,512,128]{2,1,0:T(8,128)S(1)}, f32[1,512,128]{2,1,0:T(8,128)}, u32[]{:S(2)}) copy-start(f32[1,512,128]{2,1,0:T(8,128)} %param.10) | copy-start | bytes 786436
  4.1 0.9 %copy-start.3 = (f32[1,512,128]{2,1,0:T(8,128)S(1)}, f32[1,512,128]{2,1,0:T(8,128)}, u32[]{:S(2)}) copy-start(f32[1,512,128]{2,1,0:T(8,128)} %param.11) | copy-start | bytes 786436
  5.1 0.9 %copy-start.4 = (f32[512,128]{1,0:T(8,128)S(1)}, f32[512,128]{1,0:T(8,128)}, u32[]{:S(2)}) copy-start(f32[512,128]{1,0:T(8,128)} %global_params.1) | copy-start | bytes 786436
  6.0 0.9 %copy-start.5 = (f32[512,128]{1,0:T(8,128)S(1)}, f32[512,128]{1,0:T(8,128)}, u32[]{:S(2)}) copy-start(f32[512,128]{1,0:T(8,128)} %outer_mom.1) | copy-start | bytes 786436
  7.0 0.8 %copy-start.6 = (bf16[1,256,128]{2,1,0:T(8,128)(2,1)S(1)}, bf16[1,256,128]{2,1,0:T(8,128)(2,1)}, u32[]{:S(2)}) copy-start(bf16[1,256,128]{2,1,0:T(8,128)(2,1)} %param.8) | copy-start | bytes 196612

commit v2 on v1

v2 whole, which is shorter than its diff:
```python
import functools

import jax
import jax.numpy as jnp
from jax import lax
from jax.experimental import pallas as pl
from jax.experimental.pallas import tpu as pltpu
from jax.sharding import PartitionSpec as P

INNER_STEP = 100


beta_one = 0.9
beta_two = 0.95
epsilon = 1e-08
inner_rate = 0.001
decay_rate = 0.1
outer_rate = 0.7
momentum = 0.9
mixing = 0.5

CODE_SCALE = 4096.0
LAGS = (0, 0, 2, 2)
VMEM_LIMIT = 60 * 2**20


def encode(value):
    scaled = value * CODE_SCALE
    return (scaled * jnp.abs(scaled) * (scaled * scaled)).astype(jnp.bfloat16)


def decode(coded):
    wide = coded.astype(jnp.float32)
    size = jnp.maximum(jnp.abs(wide), 1e-37)
    root = lax.rsqrt(lax.rsqrt(size)) * (1.0 / CODE_SCALE)
    return jnp.where(wide < 0.0, -root, root)


def adam(params, adam_m, adam_v, gradient):
    first_moment = beta_one * adam_m + (1.0 - beta_one) * gradient
    second_moment = beta_two * adam_v + (1.0 - beta_two) * gradient * gradient
    first_hat = first_moment / (1.0 - beta_one**INNER_STEP)
    second_hat = second_moment / (1.0 - beta_two**INNER_STEP)
    inner = params - inner_rate * (
        first_hat / (jnp.sqrt(second_hat) + epsilon) + decay_rate * params
    )
    return first_moment, second_moment, inner


def kernel(
    ring, pairs, chunks, lags,
    acts_hbm, grad_hbm, params_hbm, m_hbm, v_hbm, global_hbm, mom_hbm,
    mixed_hbm, first_hbm, second_hbm, new_global_hbm, new_mom_hbm, forward_hbm,
    mixed, first_out, second_out, new_global, new_mom, forward,
    acts, grad_out, params, adam_m, adam_v, global_params, outer_mom,
    part, r_out, r_in, inner, core_in, y_out, y_in,
    a_sem, i_sem, o_sem, w_sem, r_ss, r_rs, c_ss, c_rs, y_ss, y_rs, g_ss, g_rs,
):
    rows = params.shape[0]
    step = rows // chunks
    half = step // 2
    depth = ring // 2
    me = lax.axis_index("fsdp")
    isle = lax.axis_index("island")
    zi, xi = me // 2, lax.rem(me, 2)
    place = zi * (1 - xi) + (ring - 1 - zi) * xi
    pair, core = isle // 2, lax.rem(isle, 2)

    def index(k):
        spot = lax.rem(place + (k % ring), ring)
        side = spot // depth
        return (spot * (1 - side) + (ring - 1 - spot) * side) * 2 + side

    ahead = {"fsdp": index(1), "island": isle}
    behind = {"fsdp": index(-1), "island": isle}
    mate = {"fsdp": me, "island": pair * 2 + 1 - core}
    toward = (ahead, behind)

    def across(e, k):
        return {"fsdp": me, "island": lax.rem(pair + e, pairs) * 2 + k}

    barrier = pltpu.get_barrier_semaphore()
    peers = [ahead, behind, mate] + [across(e, k) for e in range(1, pairs) for k in range(2)]
    for peer in peers:
        pl.semaphore_signal(barrier, inc=1, device_id=peer, device_id_type=pl.DeviceIdType.MESH)

    def columns(k):
        return pl.ds(pl.multiple_of(index(k) * rows, rows), rows)

    def load(k):
        return pltpu.make_async_copy(
            acts_hbm.at[:, columns(k)], acts.at[k % ring], a_sem.at[k % ring]
        )

    singles = [
        (grad_hbm, grad_out), (params_hbm, params), (m_hbm, adam_m), (v_hbm, adam_v),
        (global_hbm, global_params), (mom_hbm, outer_mom),
    ]
    inputs = [pltpu.make_async_copy(s, d, i_sem.at[n]) for n, (s, d) in enumerate(singles)]
    needs = [depth]
    for k in range(depth - 1, 0, -1):
        needs += [k, ring - k]
    needs.append(0)
    inputs[0].start()
    for k in needs:
        load(k).start()
    for copy in inputs[1:]:
        copy.start()

    def product(k):
        load(k).wait()
        part[k] = lax.dot_general(
            acts[k], grad_out[...],
            (((0,), (0,)), ((), ())), preferred_element_type=jnp.float32,
        )

    def remote(src, dst, ss, rs, where):
        return pltpu.make_async_remote_copy(
            src_ref=src, dst_ref=dst, send_sem=ss, recv_sem=rs,
            device_id=where, device_id_type=pl.DeviceIdType.MESH,
        )

    def reach(c, q):
        return depth - (c + q) % 2

    def piece(c):
        return pl.ds(c * step, step)

    def r_copy(c, q, s):
        return remote(
            r_out.at[c, q, s], r_in.at[c, q, s], r_ss.at[c, q, s], r_rs.at[c, q, s], toward[q]
        )

    def c_copy(c):
        return remote(inner.at[piece(c)], core_in.at[c], c_ss.at[c], c_rs.at[c], mate)

    def y_copy(c, e, k):
        return remote(
            y_out.at[c, pl.ds(pl.multiple_of(core * half, half), half)],
            y_in.at[c, e, core], y_ss.at[c, e, k], y_rs.at[c, e, core], across(e, k),
        )

    def y_recv(c, e, k):
        return remote(
            y_out.at[c, pl.ds(0, half)], y_in.at[c, e, k],
            y_ss.at[c, e, k], y_rs.at[c, e, k], mate,
        )

    def g_copy(c, q, s, hop):
        k = hop if q else -hop
        first = pl.multiple_of(index(k) * rows + c * step, step)
        block = forward.at[pl.ds(first, step)]
        return remote(block, block, g_ss.at[c, q, s], g_rs.at[c, q, s], toward[q])

    landing = (
        (first_out, first_hbm), (second_out, second_hbm),
        (mixed, mixed_hbm), (new_global, new_global_hbm), (new_mom, new_mom_hbm),
    )

    def store(c, n):
        src, dst = landing[n]
        return pltpu.make_async_copy(src.at[piece(c)], dst.at[piece(c)], o_sem.at[c, n])

    def keep(c, q, hop):
        first = pl.multiple_of(index(hop if q else -hop) * rows + c * step, step)
        place_of = pl.ds(first, step)
        return pltpu.make_async_copy(
            forward.at[place_of], forward_hbm.at[place_of], w_sem.at[c, q, hop]
        )

    def sum_on(c, q, s):
        k = reach(c, q) - s
        value = part[(-k if q else k) % ring, piece(c)]
        if s > 0:
            r_copy(c, q, s - 1).wait_recv()
            value = value + decode(r_in[c, q, s - 1])
        r_out[c, q, s] = encode(value)
        r_copy(c, q, s).start()

    def reduce(c):
        total = part[0, piece(c)]
        for q in range(2):
            last = reach(c, q) - 1
            r_copy(c, q, last).wait_recv()
            total = total + decode(r_in[c, q, last])
        s = piece(c)
        first, second, own = adam(params[s], adam_m[s], adam_v[s], total)
        inner[s] = own
        c_copy(c).start()
        first_out[s] = first
        second_out[s] = second
        store(c, 0).start()
        store(c, 1).start()

    def join(c):
        c_copy(c).wait_recv()
        y_out[c] = inner[piece(c)] + core_in[c]
        for e in range(1, pairs):
            for k in range(2):
                y_copy(c, e, k).start()

    def outer(c):
        for e in range(1, pairs):
            for k in range(2):
                y_recv(c, e, k).wait_recv()
        for k in range(2):
            s = pl.ds(c * step + k * half, half)
            summed = y_out[c, pl.ds(k * half, half)]
            for e in range(1, pairs):
                summed = summed + y_in[c, e, k]
            delta = global_params[s] - summed / (2 * pairs)
            fresh = momentum * outer_mom[s] + delta
            moved = global_params[s] - outer_rate * (delta + momentum * fresh)
            merged = mixing * inner[s] + (1.0 - mixing) * moved
            first = pl.multiple_of(me * rows + c * step + k * half, half)
            forward[pl.ds(first, half)] = merged.astype(jnp.bfloat16)
            mixed[s] = merged
            new_mom[s] = fresh
            new_global[s] = moved
        for q in range(2):
            g_copy(c, q, 0, 0).start()
        keep(c, 0, 0).start()
        for n in range(2, 5):
            store(c, n).start()

    def pass_on(c, q, s):
        g_copy(c, q, s - 1, s).wait_recv()
        g_copy(c, q, s, s).start()
        keep(c, q, s).start()

    def tick(c, t):
        if t < depth:
            for q in range(2):
                if t < reach(c, q):
                    sum_on(c, q, t)
        elif t == depth:
            reduce(c)
        elif t == depth + 1:
            join(c)
        elif t == depth + 2:
            outer(c)
        else:
            for q in range(2):
                if t - depth - 2 < reach(c, q):
                    pass_on(c, q, t - depth - 2)

    inputs[0].wait()
    product(depth)
    pl.semaphore_wait(barrier, len(peers))
    for t in range(2 * depth + 2 + max(lags)):
        if t < depth - 1:
            product(depth - 1 - t)
            product(depth + 1 + t)
        elif t == depth - 1:
            product(0)
            for copy in inputs[1:]:
                copy.wait()
        for c in range(chunks):
            if 0 <= t - lags[c] < 2 * depth + 2:
                tick(c, t - lags[c])

    for c in range(chunks):
        c_copy(c).wait_send()
        for e in range(1, pairs):
            for k in range(2):
                y_copy(c, e, k).wait_send()
        for q in range(2):
            for s in range(reach(c, q)):
                r_copy(c, q, s).wait_send()
                g_copy(c, q, s, s).wait_send()
            g_copy(c, q, reach(c, q) - 1, reach(c, q)).wait_recv()
            keep(c, q, reach(c, q)).start()
    for c in range(chunks):
        for n in range(5):
            store(c, n).wait()
        keep(c, 0, 0).wait()
        for q in range(2):
            for hop in range(1, reach(c, q) + 1):
                keep(c, q, hop).wait()


def write_out(*refs):
    count = len(refs) // 2
    copies = [
        pltpu.make_async_copy(refs[n], refs[count + n], refs[-1].at[n]) for n in range(count)
    ]
    for copy in copies:
        copy.start()
    for copy in copies:
        copy.wait()


def fused(acts, grad_out, params, adam_m, adam_v, global_params, outer_mom):
    ring, islands = lax.axis_size("fsdp"), lax.axis_size("island")
    depth, pairs = ring // 2, islands // 2
    rows, width = params.shape[1:]
    tokens = acts.shape[1]
    chunks = len(LAGS)
    step = rows // chunks
    single = jax.ShapeDtypeStruct((rows, width), jnp.float32)
    whole = jax.ShapeDtypeStruct((ring * rows, width), jnp.bfloat16)
    dma = pltpu.SemaphoreType.DMA
    hbm = pl.BlockSpec(memory_space=pltpu.HBM)
    own = pltpu.VMEM((rows, width), jnp.float32)
    coded = pltpu.VMEM((chunks, 2, depth, step, width), jnp.bfloat16)
    results = pl.pallas_call(
        functools.partial(kernel, ring, pairs, chunks, LAGS),
        out_shape=[single] * 5 + [whole],
        in_specs=[hbm] * 7,
        out_specs=[hbm] * 6,
        scratch_shapes=[
            own, own, own, own, own,
            pltpu.VMEM((ring * rows, width), jnp.bfloat16),
            pltpu.VMEM((ring, tokens, rows), jnp.bfloat16),
            pltpu.VMEM((tokens, width), jnp.bfloat16),
            own, own, own, own, own,
            pltpu.VMEM((ring, rows, width), jnp.float32),
            coded, coded,
            own,
            pltpu.VMEM((chunks, step, width), jnp.float32),
            pltpu.VMEM((chunks, step, width), jnp.float32),
            pltpu.VMEM((chunks, pairs, 2, step // 2, width), jnp.float32),
            dma((ring,)), dma((6,)), dma((chunks, 5)), dma((chunks, 2, depth + 1)),
            dma((chunks, 2, depth)), dma((chunks, 2, depth)),
            dma((chunks,)), dma((chunks,)),
            dma((chunks, pairs, 2)), dma((chunks, pairs, 2)),
            dma((chunks, 2, depth)), dma((chunks, 2, depth)),
        ],
        compiler_params=pltpu.CompilerParams(
            collective_id=0, has_side_effects=True, vmem_limit_bytes=VMEM_LIMIT
        ),
    )(acts[0], grad_out[0], params[0], adam_m[0], adam_v[0], global_params, outer_mom)
    mixed, first, second, new_global, new_mom, forward = pl.pallas_call(
        write_out,
        out_shape=[single] * 5 + [whole],
        in_specs=[hbm] * 6,
        out_specs=[hbm] * 6,
        scratch_shapes=[dma((6,))],
        compiler_params=pltpu.CompilerParams(vmem_limit_bytes=VMEM_LIMIT),
    )(*results)
    return mixed[None], first[None], second[None], new_global, new_mom, forward[None]


def general(acts, grad_out, params, adam_m, adam_v, global_params, outer_mom):
    shard_rows = params.shape[1]
    features = acts.shape[2]
    padded_rows = shard_rows * lax.axis_size("fsdp")
    islands = lax.axis_size("island")
    inputs = acts[0]
    cotangent = grad_out[0]
    whole = jnp.einsum("td,th->dh", inputs, cotangent, preferred_element_type=jnp.float32)
    whole = jnp.pad(whole, ((0, padded_rows - features), (0, 0)))
    gradient = lax.psum_scatter(whole, "fsdp", scatter_dimension=0, tiled=True)
    first_moment, second_moment, inner = adam(params, adam_m, adam_v, gradient[None])
    summed = lax.psum(inner, "island")
    delta = global_params - summed[0] / islands
    new_mom = momentum * outer_mom + delta
    new_global = global_params - outer_rate * (delta + momentum * new_mom)
    mixed = mixing * inner + (1.0 - mixing) * new_global[None]
    gathered = lax.all_gather(mixed.astype(jnp.bfloat16), "fsdp", axis=1, tiled=True)
    forward_weight = gathered[:, :features]
    return (mixed, first_moment, second_moment, new_global, new_mom, forward_weight)


def on_device(acts, *others):
    fsdp, islands = lax.axis_size("fsdp"), lax.axis_size("island")
    rows = others[1].shape[1]
    fits = (
        rows * fsdp == acts.shape[2]
        and rows % (len(LAGS) * 128) == 0
        and fsdp % 2 == 0
        and 2 <= fsdp // 2 <= 4
        and islands == 4
    )
    return (fused if fits else general)(acts, *others)


def solution(mesh):
    in_specs = (
        P("island", "fsdp", None),
        P("island", "fsdp", None),
        P("island", "fsdp", None),
        P("island", "fsdp", None),
        P("island", "fsdp", None),
        P("fsdp", None),
        P("fsdp", None),
    )
    out_specs = (
        P("island", "fsdp", None),
        P("island", "fsdp", None),
        P("island", "fsdp", None),
        P("fsdp", None),
        P("fsdp", None),
        P("island", None, None),
    )
    return jax.shard_map(
        on_device, mesh=mesh, in_specs=in_specs, out_specs=out_specs, check_vma=False
    )
```

time: 57.7 us -> 119 us (2.06)
  Pallas kernels: 45 us -> 118 us
  local copies, waits for them, and re-layouts: 11.7 us -> 0 us
    pallas_call x1 -> x2, Pallas kernels: 45 us -> 118 us  [the longest x1 72.6 us: fused(): pl.pallas_call(write_out, out_shape=[single] * 5 + [whole], in_specs=[hbm...]
    unnamed x20 -> x0, local copies, waits for them, and re-layouts: 11.7 us -> none
where the time goes in v2:
time: 119 us
  Pallas kernels  118 us (99%)
    pallas_call x1, Pallas kernels, fused(): pl.pallas_call(write_out, out_shape=[single] * 5 + [whole], in_specs=[hbm...  72.6 us
    pallas_call x1, Pallas kernels, fused(): pl.pallas_call(functools.partial(kernel, ring, pairs, chunks, LAGS), out_...  45.8 us

profile of v2, /device:TPU:0, one launch (start us, length us, event | category | flops | bytes accessed | tf_op | source)
XLA Modules:
  0.0 119.1 jit_solution(18218972516488308034)
XLA Ops:
  0.6 45.8 %shard_map.118 = (f32[512,128]{1,0:T(8,128)}, f32[512,128]{1,0:T(8,128)}, f32[512,128]{1,0:T(8,128)}, f32[512,128]{1,0:T(8,128)}, f32[512,128]{1,0:T(8,128)}, /*index=5*/bf16[4096,128]{1,0:T(8,128)(2,1)}) custom-call(bf16[256,4096]{1,0:T(8,128)(2,1)} %bitcast.9, bf16[256,128]{1,0:T(8,128)(2,1)} %bitcast.13, f32[512,128]{1,0:T(8,128)} %bitcast.10, ...), custom_call_target="tpu_custom_call" | custom-call | tf_op jit(solution)/shard_map/pallas_call | solution.py:306
  46.4 72.6 %shard_map.119 = (f32[512,128]{1,0:T(8,128)}, f32[512,128]{1,0:T(8,128)}, f32[512,128]{1,0:T(8,128)}, f32[512,128]{1,0:T(8,128)}, f32[512,128]{1,0:T(8,128)}, /*index=5*/bf16[4096,128]{1,0:T(8,128)(2,1)}) custom-call(f32[512,128]{1,0:T(8,128)} %get-tuple-element.18.refs_0_, f32[512,128]{1,0:T(8,128)} %get-tuple-element.19.refs_1_, ...), custom_call_target="tpu_custom_call" | custom-call | tf_op jit(solution)/shard_map/pallas_call | solution.py:333
